TPU v7x, 256 devices: a whole 4x4x8 slice. The times are simulated.
256 devices in a mesh: tok: 32 (over y, z), wi: 2 (over x_lo), wo: 4 (over x_hi, core).
Axes of the slice: x: 4 (x_hi: 2, x_lo: 2; x = x_hi * 2 + x_lo), y: 4, z: 8, core: 2. Of those that a mesh axis runs over, the one named last changes fastest.
Arguments:
- tokens: bfloat16 [128, 8192], P(('tok', 'wo'), 'wi'), may hold values from -6 to 6
- gate_weight: bfloat16 [28672, 8192], P(('tok', 'wo'), 'wi'), may hold values from -0.0625 to 0.0625
- up_weight: bfloat16 [28672, 8192], P(('tok', 'wo'), 'wi'), may hold values from -0.0625 to 0.0625
- down_weight: bfloat16 [28672, 8192], P(('tok', 'wo'), 'wi'), may hold values from -0.03125 to 0.03125
- cotangent: bfloat16 [128, 8192], P(('tok', 'wo'), 'wi'), may hold values from -6 to 6
Outputs:
- output: bfloat16 [128, 8192], P(('tok', 'wo'), 'wi')
- grad_input: bfloat16 [128, 8192], P(('tok', 'wo'), 'wi')
- grad_gate: bfloat16 [28672, 8192], P(('tok', 'wo'), 'wi')
- grad_up: bfloat16 [28672, 8192], P(('tok', 'wo'), 'wi')
- grad_down: bfloat16 [28672, 8192], P(('tok', 'wo'), 'wi')
All inputs are finite; a program needn't handle non-finite values.
Results may differ from a plain program's by a relative error of at most 0.02.
Values may be sent and summed in bfloat16 or wider, within the bound.
A program may use at most 64 MiB of HBM per device.

v0:
```python
import jax
import jax.numpy as jnp
from jax import lax
from jax.sharding import PartitionSpec as P


def spread(term_fn, rows):
    return lax.psum_scatter(
        term_fn(jnp.int32(0), rows * lax.axis_size(("tok", "wo"))),
        ("tok", "wo"),
        scatter_dimension=0,
        tiled=True,
    )


def contract_first(left, right):
    return lax.dot_general(
        left, right, (((0,), (0,)), ((), ())), preferred_element_type=jnp.float32
    )


def contract_last(left, right):
    return lax.dot_general(
        left, right, (((1,), (1,)), ((), ())), preferred_element_type=jnp.float32
    )


def per_device(tokens, gate_weight, up_weight, down_weight, cotangent):
    rows = tokens.shape[0]
    whole = lax.all_gather(tokens, ("tok", "wo"), axis=0, tiled=True)
    gate_part = contract_last(gate_weight, whole)
    up_part = contract_last(up_weight, whole)
    gate, up = (
        lax.psum(gate_part.astype(jnp.bfloat16), "wi").astype(jnp.float32),
        lax.psum(up_part.astype(jnp.bfloat16), "wi").astype(jnp.float32),
    )
    sig = jax.nn.sigmoid(gate)
    act = gate * sig
    hidden = (act * up).astype(jnp.bfloat16)

    def forward_term(start, count):
        return contract_first(hidden, down_weight)

    output = spread(forward_term, rows).astype(jnp.bfloat16)
    cot_whole = lax.all_gather(cotangent, ("tok", "wo"), axis=0, tiled=True)
    dhid = lax.psum(contract_last(down_weight, cot_whole).astype(jnp.bfloat16), "wi").astype(
        jnp.float32
    )
    dgate = (dhid * up * sig * (1.0 + gate * (1.0 - sig))).astype(jnp.bfloat16)
    dup = (dhid * act).astype(jnp.bfloat16)
    grad_down = jnp.dot(hidden, cot_whole, preferred_element_type=jnp.float32).astype(jnp.bfloat16)
    grad_gate = jnp.dot(dgate, whole, preferred_element_type=jnp.float32).astype(jnp.bfloat16)
    grad_up = jnp.dot(dup, whole, preferred_element_type=jnp.float32).astype(jnp.bfloat16)

    def backward_term(start, count):
        return contract_first(dgate, gate_weight) + contract_first(dup, up_weight)

    grad_input = spread(backward_term, rows).astype(jnp.bfloat16)
    return (output, grad_input, grad_gate, grad_up, grad_down)


def solution(mesh):
    in_specs = (
        P(("tok", "wo"), "wi"),
        P(("tok", "wo"), "wi"),
        P(("tok", "wo"), "wi"),
        P(("tok", "wo"), "wi"),
        P(("tok", "wo"), "wi"),
    )
    out_specs = (
        P(("tok", "wo"), "wi"),
        P(("tok", "wo"), "wi"),
        P(("tok", "wo"), "wi"),
        P(("tok", "wo"), "wi"),
        P(("tok", "wo"), "wi"),
    )
    return jax.shard_map(
        per_device, mesh=mesh, in_specs=in_specs, out_specs=out_specs, check_vma=False
    )
```

profile of v0, /device:TPU:1, one launch (start us, length us, event | category | flops | bytes accessed | tf_op | source)
XLA Modules:
  0.0 989.6 jit_solution(1717061471684818860)
XLA Ops:
  7.2 0.0 copy-start
  7.2 0.0 all-gather.5.cloned.1.call-start
  7.2 0.7 all-gather.5.cloned.1.call-update
  7.9 0.0 all-gather.7.cloned.1.call-start
  8.0 0.7 all-gather.7.cloned.1.call-update
  8.7 0.0 all-reduce.7.cloned.1.call-start
  8.7 122.3 %all-gather.5.cloned.1.call-done = bf16[128,1,4096]{2,1,0:T(2,128)(2,1)} async-done(((bf16[1,1,4096]{2,1,0:T(2,128)(2,1)}), bf16[128,1,4096]{2,1,0:T(2,128)(2,1)}) %all-gather.5.cloned.1.call-update) | async-done | bytes 1048592 | tf_op jit(solution)/shard_map/all_gather | solution.py:30
  131.0 0.0 copy-start.3
  131.0 2.9 copy.10
  133.9 0.0 copy-done.3
  133.9 0.0 copy-start.1
  133.9 1.3 convolution_convert_fusion.4
  135.2 0.2 copy-done.1
  135.4 1.3 convolution_convert_fusion.5
  136.7 0.0 copy-start.8
  136.7 109.9 %all-gather.7.cloned.1.call-done = bf16[128,1,4096]{2,1,0:T(2,128)(2,1)} async-done(((bf16[1,1,4096]{2,1,0:T(2,128)(2,1)}), bf16[128,1,4096]{2,1,0:T(2,128)(2,1)}) %all-gather.7.cloned.1.call-update) | async-done | bytes 1048592 | tf_op jit(solution)/shard_map/all_gather | solution.py:45
  246.6 0.0 copy-done
  246.6 3.7 convolution_convert_fusion.3
  250.3 0.0 all-reduce.7.cloned.1.call-update
  250.3 0.0 copy-done.8
  250.3 0.6 dynamic-slice
  251.0 29.6 %all-reduce.7.cloned.1.call-done = (bf16[224,128]{1,0:T(8,128)(2,1)}, bf16[224,128]{1,0:T(8,128)(2,1)}, bf16[224,128]{1,0:T(8,128)(2,1)}) async-done(((bf16[224,128]{1,0:T(8,128)(2,1)}, bf16[224,128]{1,0:T(8,128)(2,1)}, bf16[224,128]{1,0:T(8,128)(2,1)}), (bf16[224,128]{1,0:T(8,128)(2,1)}, bf16[224,128]{1,0:T(8,128)(2,1)}, bf16[224,128]{1,0:T(8,128)(2,1)})) %all-reduce.7.cloned.1.call-update) | async-done | bytes 172048 | tf_op jit(solution)/shard_map/psum | solution.py:35
  280.6 0.0 copy-start.2
  280.6 0.0 copy-start.5
  280.6 0.0 copy-start.6
  280.6 0.0 copy-start.7
  280.6 2.8 fusion.20
  283.4 0.0 copy-done.2
  283.4 0.0 copy-done.5
  283.4 0.0 copy-done.6
  283.4 0.0 copy-done.7
  283.4 0.5 fusion.23
  283.9 1.9 convolution_convert_fusion.2
  285.8 0.0 copy-start.4
  285.8 1.9 convolution_convert_fusion.1
  287.7 0.0 copy-done.4
  287.7 1.9 convolution_add_fusion
  289.6 687.0 %all-reduce.8 = (bf16[128,4096]{1,0:T(8,128)(2,1)S(1)}, bf16[128,4096]{1,0:T(8,128)(2,1)}) all-reduce(f32[128,4096]{1,0:T(8,128)} %fusion.20, f32[128,4096]{1,0:T(8,128)} %convolution_add_fusion), channel_id=2, replica_groups=mesh['tok'=32,'wi'=2,'wo'=4] {'tok','wo'}, use_global_device_ids=true, to_apply=%region_2.0.clone | all-reduce | flops 1048576 | bytes 6291456
  976.6 2.1 dynamic-slice_convert_fusion
  978.7 4.4 convolution_convert_fusion
Async XLA Ops:
  7.2 239.4 %copy-start = (bf16[224,4096]{1,0:T(8,128)(2,1)S(1)}, bf16[224,4096]{1,0:T(8,128)(2,1)}, u32[]{:S(2)}) copy-start(bf16[224,4096]{1,0:T(8,128)(2,1)} %param.8) | copy-start | bytes 5505028
  7.2 123.8 %all-gather.5.cloned.1.call-start = ((), (), s32[]{:S(2)}) async-start(), calls=%async_computation | async-start | bytes 2113536 | tf_op jit(solution)/shard_map/all_gather | solution.py:30
  7.9 238.7 %all-gather.7.cloned.1.call-start = ((), (), s32[]{:S(2)}) async-start(), calls=%async_computation.1 | async-start | bytes 2113536 | tf_op jit(solution)/shard_map/all_gather | solution.py:45
  8.7 271.9 %all-reduce.7.cloned.1.call-start = ((), (), s32[]{:S(2)}) async-start(), calls=%async_computation.2 | async-start | bytes 344064 | tf_op jit(solution)/shard_map/psum | solution.py:35
  131.0 2.9 copy-start.3
  133.9 1.5 copy-start.1
  136.7 113.7 %copy-start.8 = (u32[256]{0:T(256)S(1)}, u32[256]{0:T(256)}, u32[]{:S(2)}) copy-start(u32[256]{0:T(256)} %constant.9) | copy-start | bytes 3076
  280.6 2.8 copy-start.2
  280.6 2.8 copy-start.5
  280.6 2.8 copy-start.6
  280.6 2.8 copy-start.7
  285.8 1.9 copy-start.4
Sparse Core Ops, SparseCore 0:
  11.6 119.3 all-gather.4
  134.6 111.9 all-gather.6
  250.5 30.0 all-reduce.6
where the time goes:
time: 995 us; the launch traced here: 990 us
  blocking collectives  687 us (69%)
  waiting for transfers between devices  263 us (26%)
  matrix products  19.6 us (2%)
  between operations  13.8 us (1%)
    unnamed x1, blocking collectives  687 us
    all_gather x1, waiting for transfers between devices, per_device(): whole = lax.all_gather(tokens, ('tok', 'wo'), axis=0, tiled=True)  122 us
    all_gather x1, waiting for transfers between devices, per_device(): cot_whole = lax.all_gather(cotangent, ('tok', 'wo'), axis=0, tiled=True)  110 us
    psum x1, waiting for transfers between devices, per_device(): lax.psum(up_part.astype(jnp.bfloat16), 'wi').astype(jnp.float32)  29.6 us
  transfers between devices with their start and end apart: 3, of which 3 were waited for; matrix products, arithmetic and copies ran while one was open for 1% of the time, Pallas kernels for 0%

commit v1 on v0

v1 whole, which is shorter than its diff:
```python
import functools

import jax
import jax.numpy as jnp
from jax import lax
from jax.experimental import pallas as pl
from jax.experimental.pallas import tpu as pltpu
from jax.sharding import PartitionSpec as P

MESH = pl.DeviceIdType.MESH
BF = jnp.bfloat16
F32 = jnp.float32
NY, NZ, NX, NC = 4, 8, 2, 2
ROW = NZ * NX
HALF = NY * ROW


def nt(left, right):
    return lax.dot_general(left, right, (((1,), (1,)), ((), ())), preferred_element_type=F32)


def nn(left, right):
    return jnp.dot(left, right, preferred_element_type=F32)


def exchange_kernel(
    tok_ref, cot_ref, gw_hbm, uw_hbm, dw_hbm,
    all_out, act_out, rows_out,
    wv, own32, own, zxb, whole, wis, wir, tp, cs, cr, mine, ys, yr, zs, zr, acts,
    w_sem, zx_s, zx_r, y_s, y_r, sib_s, sib_r, wi_s, wi_r,
    c_s, c_r, ry_s, ry_r, rz_s, rz_r, out_sem,
):
    width = wv.shape[2]
    parts = width // (ROW * 128)
    wide = ROW * 128
    tok_i, wi_i, wo_i = lax.axis_index("tok"), lax.axis_index("wi"), lax.axis_index("wo")
    y, z = tok_i // NZ, lax.rem(tok_i, NZ)
    xh, c = wo_i // NC, lax.rem(wo_i, NC)
    zx = z * NX + xh

    def zx_dev(d):
        t = lax.rem(zx + d, ROW)
        return (y * NZ + t // NX, wi_i, lax.rem(t, NX) * NC + c), t

    def y_dev(d):
        t = lax.rem(y + d, NY)
        return (t * NZ + z, wi_i, wo_i), t

    sib = (tok_i, wi_i, xh * NC + (1 - c))
    pair = (tok_i, 1 - wi_i, wo_i)

    barrier = pltpu.get_barrier_semaphore()

    def greet(d, _):
        pl.semaphore_signal(barrier, inc=1, device_id=zx_dev(d)[0], device_id_type=MESH)
        return 0

    lax.fori_loop(1, ROW, greet, 0)
    for d in range(1, NY):
        pl.semaphore_signal(barrier, inc=1, device_id=y_dev(d)[0], device_id_type=MESH)
    pl.semaphore_signal(barrier, inc=1, device_id=sib, device_id_type=MESH)
    pl.semaphore_signal(barrier, inc=1, device_id=pair, device_id_type=MESH)

    loads = [
        pltpu.make_async_copy(w, wv.at[i], w_sem.at[i])
        for i, w in enumerate((gw_hbm, uw_hbm, dw_hbm))
    ]
    for load in loads:
        load.start()
    for a, ref in enumerate((tok_ref, cot_ref)):
        row = ref[...].astype(F32)
        for k in range(width // 128):
            own32[pl.ds(a * (width // 128) + k, 1), :] = row[:, k * 128 : (k + 1) * 128]
    for s in range(2 * parts):
        own[s] = own32[s * ROW : (s + 1) * ROW, :].astype(BF)
        zxb[s, zx] = own[s]
    pl.semaphore_wait(barrier, ROW - 1 + NY - 1 + 2)

    for s in range(2 * parts):

        def send(d, _, s=s):
            pltpu.make_async_remote_copy(
                src_ref=own.at[s], dst_ref=zxb.at[s, zx],
                send_sem=zx_s.at[s], recv_sem=zx_r.at[s],
                device_id=zx_dev(d)[0], device_id_type=MESH,
            ).start()
            return 0

        lax.fori_loop(1, ROW, send, 0)

    def block(ref, s, yy, cc):
        rows = pl.ds(pl.multiple_of(cc * HALF + yy * ROW, ROW), ROW)
        return ref.at[s // parts, rows, pl.ds((s % parts) * wide, wide)]

    def to_y(s, d):
        return pltpu.make_async_remote_copy(
            src_ref=block(whole, s, y, c), dst_ref=block(whole, s, y, c),
            send_sem=y_s.at[s, d - 1], recv_sem=y_r.at[s, d - 1],
            device_id=y_dev(d)[0], device_id_type=MESH,
        )

    def to_sib(s, d):
        yy = lax.rem(y + NY - d, NY)
        return pltpu.make_async_remote_copy(
            src_ref=block(whole, s, yy, c), dst_ref=block(whole, s, yy, c),
            send_sem=sib_s.at[s, d], recv_sem=sib_r.at[s, d],
            device_id=sib, device_id_type=MESH,
        )

    def gather_zx(s):
        some = zxb.at[s, pl.ds(0, ROW - 1)]
        pltpu.make_async_copy(some, some, zx_r.at[s]).wait()
        turned = jnp.swapaxes(zxb[s], 0, 1)
        rows = pl.ds(pl.multiple_of(c * HALF + y * ROW, ROW), ROW)
        for k in range(ROW):
            col = (s % parts) * wide + k * 128
            whole[s // parts, rows, pl.ds(col, 128)] = turned[k]
        for d in (2, 1, 3):
            to_y(s, d).start()
        to_sib(s, 0).start()

    def gather_y(s):
        for d in (1, 3, 2):
            to_y(s, d).wait_recv()
            to_sib(s, d).start()

    def gather_sib(s):
        for d in (0, 1, 3, 2):
            to_sib(s, d).wait_recv()

    def piece(ref, i, s):
        return ref[i, :, pl.ds((s % parts) * wide, wide)]

    def to_pair(i):
        return pltpu.make_async_remote_copy(
            src_ref=wis.at[i], dst_ref=wir.at[i], send_sem=wi_s.at[i], recv_sem=wi_r.at[i],
            device_id=pair, device_id_type=MESH,
        )

    gather_zx(0)
    gather_zx(1)
    gather_y(0)
    gather_zx(2)
    gather_y(1)
    gather_sib(0)
    loads[0].wait()
    loads[1].wait()
    gate = nt(piece(wv, 0, 0), piece(whole, 0, 0))
    up = nt(piece(wv, 1, 0), piece(whole, 0, 0))
    gather_zx(3)
    gather_y(2)
    gather_sib(1)
    gate += nt(piece(wv, 0, 1), piece(whole, 0, 1))
    wis[0] = gate.astype(BF)
    to_pair(0).start()
    up += nt(piece(wv, 1, 1), piece(whole, 0, 1))
    wis[1] = up.astype(BF)
    to_pair(1).start()
    gather_y(3)
    gather_sib(2)
    loads[2].wait()
    dhid = nt(piece(wv, 2, 2), piece(whole, 1, 2))
    gather_sib(3)
    dhid += nt(piece(wv, 2, 3), piece(whole, 1, 3))
    wis[2] = dhid.astype(BF)
    to_pair(2).start()
    saved = [pltpu.make_async_copy(whole, all_out, out_sem.at[0])]
    saved[0].start()

    to_pair(0).wait_recv()
    to_pair(1).wait_recv()
    gate = gate + wir[0].astype(F32)
    up = up + wir[1].astype(F32)
    sig = jax.nn.sigmoid(gate)
    act = gate * sig
    hidden = (act * up).astype(BF)
    acts[0] = hidden
    tp[0] = jnp.transpose(hidden.astype(F32)).astype(BF)

    rows_own = pl.ds(pl.multiple_of(c * HALF, HALF), HALF)
    rows_sib = pl.ds(pl.multiple_of((1 - c) * HALF, HALF), HALF)

    def to_core(a, h):
        return pltpu.make_async_remote_copy(
            src_ref=cs.at[a, h], dst_ref=cr.at[a, h], send_sem=c_s.at[a, h],
            recv_sem=c_r.at[a, h], device_id=sib, device_id_type=MESH,
        )

    def term(a, h):
        cols = pl.ds(h * wide, wide)
        for part, rows in ((0, rows_sib), (1, rows_own)):
            if a == 0:
                value = nn(tp[0, rows, :], wv[2, :, cols])
            else:
                value = nn(tp[1, rows, :], wv[0, :, cols]) + nn(tp[2, rows, :], wv[1, :, cols])
            if part == 0:
                cs[a, h] = value.astype(BF)
                to_core(a, h).start()
            else:
                mine[a, h] = value

    def to_row(a, h, d):
        there = pl.ds(pl.multiple_of(lax.rem(y + d, NY) * ROW, ROW), ROW)
        return pltpu.make_async_remote_copy(
            src_ref=ys.at[a, h, there], dst_ref=yr.at[a, h, d - 1], send_sem=ry_s.at[a, h, d - 1],
            recv_sem=ry_r.at[a, h, d - 1], device_id=y_dev(d)[0], device_id_type=MESH,
        )

    def scatter_core(a, h):
        to_core(a, h).wait_recv()
        value = mine[a, h] + cr[a, h].astype(F32)
        mine[a, h] = value
        ys[a, h] = value.astype(BF)
        for d in (2, 1, 3):
            to_row(a, h, d).start()

    def scatter_y(a, h):
        here = pl.ds(pl.multiple_of(y * ROW, ROW), ROW)
        value = mine[a, h, here]
        for d in (1, 3, 2):
            to_row(a, h, d).wait_recv()
            value = value + yr[a, h, d - 1].astype(F32)
        value = value.astype(BF)
        split = jnp.concatenate(
            [value[:, k * 128 : (k + 1) * 128].reshape(1, ROW, 128) for k in range(ROW)], axis=0
        )
        zs[a, h] = jnp.swapaxes(split, 0, 1)
        zr[a, h, 0] = zs[a, h, zx]

        def send(d, _):
            there, t = zx_dev(d)
            pltpu.make_async_remote_copy(
                src_ref=zs.at[a, h, t], dst_ref=zr.at[a, h, d], send_sem=rz_s.at[a, h],
                recv_sem=rz_r.at[a, h], device_id=there, device_id_type=MESH,
            ).start()
            return 0

        lax.fori_loop(1, ROW, send, 0)

    def scatter_zx(a, h):
        some = zr.at[a, h, pl.ds(1, ROW - 1)]
        pltpu.make_async_copy(some, some, rz_r.at[a, h]).wait()
        rows_out[a, h * ROW : (h + 1) * ROW, :] = jnp.sum(zr[a, h].astype(F32), axis=0)

    term(0, 0)
    term(0, 1)
    to_pair(2).wait_recv()
    dhid = dhid + wir[2].astype(F32)
    dgate = (dhid * up * sig * (1.0 + gate * (1.0 - sig))).astype(BF)
    dup = (dhid * act).astype(BF)
    acts[1] = dgate
    acts[2] = dup
    saved.append(pltpu.make_async_copy(acts, act_out, out_sem.at[1]))
    saved[1].start()
    tp[1] = jnp.transpose(dgate.astype(F32)).astype(BF)
    tp[2] = jnp.transpose(dup.astype(F32)).astype(BF)
    scatter_core(0, 0)
    term(1, 0)
    scatter_core(0, 1)
    term(1, 1)
    scatter_core(1, 0)
    scatter_core(1, 1)
    scatter_y(0, 0)
    scatter_y(0, 1)
    scatter_y(1, 0)
    scatter_y(1, 1)
    for a in range(2):
        for h in range(parts):
            scatter_zx(a, h)

    for s in range(2 * parts):
        some = zxb.at[s, pl.ds(0, ROW - 1)]
        pltpu.make_async_copy(some, some, zx_s.at[s]).wait()
        for d in range(1, NY):
            to_y(s, d).wait_send()
        for d in range(NY):
            to_sib(s, d).wait_send()
    for i in range(3):
        to_pair(i).wait_send()
    for a in range(2):
        for h in range(parts):
            to_core(a, h).wait_send()
            for d in range(1, NY):
                to_row(a, h, d).wait_send()
            some = zs.at[a, h, pl.ds(0, ROW - 1)]
            pltpu.make_async_copy(some, some, rz_s.at[a, h]).wait()
    for copy in saved:
        copy.wait()


def grads_kernel(all_ref, act_ref, rows_ref, out_ref, gin_ref, gg_ref, gu_ref, gd_ref):
    gd_ref[...] = nn(act_ref[0], all_ref[1]).astype(BF)
    gg_ref[...] = nn(act_ref[1], all_ref[0]).astype(BF)
    gu_ref[...] = nn(act_ref[2], all_ref[0]).astype(BF)

    @pl.when(pl.program_id(0) == 0)
    def _():
        for a, ref in enumerate((out_ref, gin_ref)):
            for k in range(rows_ref.shape[1]):
                ref[:, k * 128 : (k + 1) * 128] = rows_ref[a, k : k + 1, :].astype(BF)


def per_device(tokens, gate_weight, up_weight, down_weight, cotangent):
    units, width = gate_weight.shape
    tokens_all = ROW * NY * NC
    wide = ROW * 128
    parts = width // wide
    st = 2 * parts
    vm = pl.BlockSpec(memory_space=pltpu.VMEM)
    hbm = pl.BlockSpec(memory_space=pl.ANY)
    sem = pltpu.SemaphoreType.DMA
    whole, acts, rows = pl.pallas_call(
        exchange_kernel,
        out_shape=[
            jax.ShapeDtypeStruct((2, tokens_all, width), BF),
            jax.ShapeDtypeStruct((3, units, tokens_all), BF),
            jax.ShapeDtypeStruct((2, width // 128, 128), F32),
        ],
        in_specs=[vm, vm, hbm, hbm, hbm],
        out_specs=[hbm, hbm, vm],
        scratch_shapes=[
            pltpu.VMEM((3, units, width), BF),
            pltpu.VMEM((2 * width // 128, 128), F32),
            pltpu.VMEM((st, ROW, 128), BF),
            pltpu.VMEM((st, ROW, ROW, 128), BF),
            pltpu.VMEM((2, tokens_all, width), BF),
            pltpu.VMEM((3, units, tokens_all), BF),
            pltpu.VMEM((3, units, tokens_all), BF),
            pltpu.VMEM((3, tokens_all, units), BF),
            pltpu.VMEM((2, parts, HALF, wide), BF),
            pltpu.VMEM((2, parts, HALF, wide), BF),
            pltpu.VMEM((2, parts, HALF, wide), F32),
            pltpu.VMEM((2, parts, HALF, wide), BF),
            pltpu.VMEM((2, parts, NY - 1, ROW, wide), BF),
            pltpu.VMEM((2, parts, ROW, ROW, 128), BF),
            pltpu.VMEM((2, parts, ROW, ROW, 128), BF),
            pltpu.VMEM((3, units, tokens_all), BF),
            sem((3,)), sem((st,)), sem((st,)), sem((st, NY - 1)), sem((st, NY - 1)),
            sem((st, NY)), sem((st, NY)), sem((3,)), sem((3,)),
            sem((2, parts)), sem((2, parts)), sem((2, parts, NY - 1)), sem((2, parts, NY - 1)),
            sem((2, parts)), sem((2, parts)), sem((2,)),
        ],
        compiler_params=pltpu.CompilerParams(
            collective_id=0, has_side_effects=True, vmem_limit_bytes=48 << 20
        ),
        name="exchange",
    )(tokens, cotangent, gate_weight, up_weight, down_weight)
    step = 512
    big = pl.BlockSpec((units, step), lambda j: (0, j))
    small = pl.BlockSpec((1, width), lambda j: (0, 0))
    output, grad_input, grad_gate, grad_up, grad_down = pl.pallas_call(
        grads_kernel,
        grid=(width // step,),
        out_shape=[jax.ShapeDtypeStruct((1, width), BF)] * 2
        + [jax.ShapeDtypeStruct((units, width), BF)] * 3,
        in_specs=[
            pl.BlockSpec((2, tokens_all, step), lambda j: (0, 0, j)),
            pl.BlockSpec((3, units, tokens_all), lambda j: (0, 0, 0)),
            pl.BlockSpec((2, width // 128, 128), lambda j: (0, 0, 0)),
        ],
        out_specs=[small, small, big, big, big],
        compiler_params=pltpu.CompilerParams(vmem_limit_bytes=48 << 20),
        name="grads",
    )(whole, acts, rows)
    return output, grad_input, grad_gate, grad_up, grad_down


def solution(mesh):
    spec = P(("tok", "wo"), "wi")
    return jax.shard_map(
        per_device, mesh=mesh, in_specs=(spec,) * 5, out_specs=(spec,) * 5, check_vma=False
    )
```

time: 995 us -> 71.9 us (0.07)
  blocking collectives: 687 us -> 0 us
  waiting for transfers between devices: 263 us -> 0 us
  Pallas kernels: 0 us -> 63.4 us
  matrix products: 19.6 us -> 0 us
  between operations: 13.8 us -> 0.66 us
    unnamed x1 -> x0, blocking collectives: 687 us -> none
    all_gather x2 -> x0, waiting for transfers between devices: 232 us -> none  [the longest x1 122 us: per_device(): whole = lax.all_gather(tokens, ('tok', 'wo'), axis=0, tiled=True)]
    pallas_call x0 -> x2, Pallas kernels: none -> 63.4 us  [the longest x1 58.2 us: per_device(): pl.pallas_call(exchange_kernel, out_shape=[jax.ShapeDtypeStruct((2, token...]
    psum x1 -> x0, waiting for transfers between devices: 29.6 us -> none  [per_device(): lax.psum(up_part.astype(jnp.bfloat16), 'wi').astype(jnp.float32)]
    dot_general x9 -> x0, matrix products: 19.6 us -> none  [the longest x3 6.23 us: contract_last(): lax.dot_general(left, right, (((1,), (1,)), ((), ())), preferred_element_...]
  transfers between devices with their start and end apart: 3 -> 0, of which waited for: 3 -> 0; matrix products, arithmetic and copies ran while one was open for 1% -> 0% of each run, Pallas kernels for 0% -> 0%
where the time goes in v1:
time: 71.9 us; the launch traced here: 71.6 us
  Pallas kernels  63.4 us (88%)
  local copies, waits for them, and re-layouts  7.51 us (10%)
    pallas_call x1, Pallas kernels, per_device(): pl.pallas_call(exchange_kernel, out_shape=[jax.ShapeDtypeStruct((2, token...  58.2 us
    unnamed x12, local copies, waits for them, and re-layouts  7.51 us
    pallas_call x1, Pallas kernels, per_device(): pl.pallas_call(grads_kernel, grid=(width // step,), out_shape=[jax.ShapeD...  5.15 us

profile of v1, /device:TPU:1, one launch (start us, length us, event | category | flops | bytes accessed | tf_op | source)
XLA Modules:
  0.0 71.6 jit_solution(15949091646313787212)
XLA Ops:
  0.6 0.0 copy-start.1
  0.6 1.5 %copy-done.1 = bf16[224,4096]{1,0:T(8,128)(2,1)S(1)} copy-done((bf16[224,4096]{1,0:T(8,128)(2,1)S(1)}, bf16[224,4096]{1,0:T(8,128)(2,1)}, u32[]{:S(2)}) %copy-start.1) | copy-done | bytes 1835032
  2.1 0.0 copy-start.2
  2.1 1.5 %copy-done.2 = bf16[224,4096]{1,0:T(8,128)(2,1)S(1)} copy-done((bf16[224,4096]{1,0:T(8,128)(2,1)S(1)}, bf16[224,4096]{1,0:T(8,128)(2,1)}, u32[]{:S(2)}) %copy-start.2) | copy-done | bytes 1835032
  3.6 0.0 copy-start.3
  3.6 1.5 %copy-done.3 = bf16[224,4096]{1,0:T(8,128)(2,1)S(1)} copy-done((bf16[224,4096]{1,0:T(8,128)(2,1)S(1)}, bf16[224,4096]{1,0:T(8,128)(2,1)}, u32[]{:S(2)}) %copy-start.3) | copy-done | bytes 1835032
  5.1 0.0 copy-start.4
  5.1 0.7 copy-done.4
  5.9 0.0 copy-start.5
  5.9 0.7 copy-done.5
  6.6 58.2 %exchange.1 = (bf16[2,128,4096]{2,1,0:T(8,128)(2,1)}, bf16[3,224,128]{2,1,0:T(8,128)(2,1)S(1)}, f32[2,32,128]{2,1,0:T(8,128)S(1)}) custom-call(bf16[1,4096]{1,0:T(2,128)(2,1)S(1)} %copy-done.4, bf16[1,4096]{1,0:T(2,128)(2,1)S(1)} %copy-done.5, bf16[224,4096]{1,0:T(8,128)(2,1)S(1)} %copy-done.1, bf16[224,4096]{1,0:T(8,128)(2,1)S(1)} %copy-done.2, ...), custom_call_target="tpu_custom_call" | custom-call | tf_op jit(solution)/shard_map/exchange/pallas_call | solution.py:312
  64.8 0.0 copy-start
  64.8 1.6 %copy-done = bf16[2,128,4096]{2,1,0:T(8,128)(2,1)S(1)} copy-done((bf16[2,128,4096]{2,1,0:T(8,128)(2,1)S(1)}, bf16[2,128,4096]{2,1,0:T(8,128)(2,1)}, u32[]{:S(2)}) %copy-start) | copy-done | bytes 2097176
  66.4 5.1 %grads.1 = (bf16[1,4096]{1,0:T(2,128)(2,1)}, bf16[1,4096]{1,0:T(2,128)(2,1)}, bf16[224,4096]{1,0:T(8,128)(2,1)}, bf16[224,4096]{1,0:T(8,128)(2,1)}, bf16[224,4096]{1,0:T(8,128)(2,1)}) custom-call(bf16[2,128,4096]{2,1,0:T(8,128)(2,1)S(1)} %copy-done, bf16[3,224,128]{2,1,0:T(8,128)(2,1)S(1)} %get-tuple-element.9.act_ref, ...), custom_call_target="tpu_custom_call" | custom-call | tf_op jit(solution)/shard_map/grads/pallas_call | solution.py:351
Async XLA Ops:
  0.6 1.5 %copy-start.1 = (bf16[224,4096]{1,0:T(8,128)(2,1)S(1)}, bf16[224,4096]{1,0:T(8,128)(2,1)}, u32[]{:S(2)}) copy-start(bf16[224,4096]{1,0:T(8,128)(2,1)} %gw_hbm.1) | copy-start | bytes 5505028
  2.1 1.5 %copy-start.2 = (bf16[224,4096]{1,0:T(8,128)(2,1)S(1)}, bf16[224,4096]{1,0:T(8,128)(2,1)}, u32[]{:S(2)}) copy-start(bf16[224,4096]{1,0:T(8,128)(2,1)} %uw_hbm.1) | copy-start | bytes 5505028
  3.6 1.5 %copy-start.3 = (bf16[224,4096]{1,0:T(8,128)(2,1)S(1)}, bf16[224,4096]{1,0:T(8,128)(2,1)}, u32[]{:S(2)}) copy-start(bf16[224,4096]{1,0:T(8,128)(2,1)} %dw_hbm.1) | copy-start | bytes 5505028
  5.1 0.7 %copy-start.4 = (bf16[1,4096]{1,0:T(2,128)(2,1)S(1)}, bf16[1,4096]{1,0:T(2,128)(2,1)}, u32[]{:S(2)}) copy-start(bf16[1,4096]{1,0:T(2,128)(2,1)} %tok_ref.1) | copy-start | bytes 24580
  5.9 0.7 %copy-start.5 = (bf16[1,4096]{1,0:T(2,128)(2,1)S(1)}, bf16[1,4096]{1,0:T(2,128)(2,1)}, u32[]{:S(2)}) copy-start(bf16[1,4096]{1,0:T(2,128)(2,1)} %cot_ref.1) | copy-start | bytes 24580
  64.8 1.6 %copy-start = (bf16[2,128,4096]{2,1,0:T(8,128)(2,1)S(1)}, bf16[2,128,4096]{2,1,0:T(8,128)(2,1)}, u32[]{:S(2)}) copy-start(bf16[2,128,4096]{2,1,0:T(8,128)(2,1)} %get-tuple-element.8.all_ref) | copy-start | bytes 6291460

commit v2 on v1

--- a/solution.py
+++ b/solution.py
@@ -13,6 +13,8 @@
 NY, NZ, NX, NC = 4, 8, 2, 2
 ROW = NZ * NX
 HALF = NY * ROW
+TURN_G = 1
+TURN_S = (0, 1)
 
 
 def nt(left, right):
@@ -24,11 +26,12 @@
 
 
 def exchange_kernel(
-    tok_ref, cot_ref, gw_hbm, uw_hbm, dw_hbm,
-    all_out, act_out, rows_out,
-    wv, own32, own, zxb, whole, wis, wir, tp, cs, cr, mine, ys, yr, zs, zr, acts,
+    tok_hbm, cot_hbm, gw_hbm, uw_hbm, dw_hbm,
+    out_ref, gin_ref, gg_ref, gu_ref, gd_ref,
+    raw, wv, own32, own, zxb, whole, wis, wir, tp, cs, cr, mine, ys, yr, zs, zr,
     w_sem, zx_s, zx_r, y_s, y_r, sib_s, sib_r, wi_s, wi_r,
-    c_s, c_r, ry_s, ry_r, rz_s, rz_r, out_sem,
+    c_s, c_r, ry_s, ry_r, rz_s, rz_r,
+    gq, sq, rq, uq, vq, q_s, q_r, qs_s, qs_r, qy_s, qy_r,
 ):
     width = wv.shape[2]
     parts = width // (ROW * 128)
@@ -49,6 +52,18 @@
     sib = (tok_i, wi_i, xh * NC + (1 - c))
     pair = (tok_i, 1 - wi_i, wo_i)
 
+    loads = [
+        pltpu.make_async_copy(w, there, w_sem.at[i])
+        for i, (w, there) in enumerate(
+            (
+                (gw_hbm, wv.at[0]), (uw_hbm, wv.at[1]), (dw_hbm, wv.at[2]),
+                (tok_hbm, raw.at[0]), (cot_hbm, raw.at[1]),
+            )
+        )
+    ]
+    for i in (3, 4, 0, 1, 2):
+        loads[i].start()
+
     barrier = pltpu.get_barrier_semaphore()
 
     def greet(d, _):
@@ -61,14 +76,9 @@
     pl.semaphore_signal(barrier, inc=1, device_id=sib, device_id_type=MESH)
     pl.semaphore_signal(barrier, inc=1, device_id=pair, device_id_type=MESH)
 
-    loads = [
-        pltpu.make_async_copy(w, wv.at[i], w_sem.at[i])
-        for i, w in enumerate((gw_hbm, uw_hbm, dw_hbm))
-    ]
-    for load in loads:
-        load.start()
-    for a, ref in enumerate((tok_ref, cot_ref)):
-        row = ref[...].astype(F32)
+    for a in range(2):
+        loads[3 + a].wait()
+        row = raw[a].astype(F32)
         for k in range(width // 128):
             own32[pl.ds(a * (width // 128) + k, 1), :] = row[:, k * 128 : (k + 1) * 128]
     for s in range(2 * parts):
@@ -76,7 +86,20 @@
         zxb[s, zx] = own[s]
     pl.semaphore_wait(barrier, ROW - 1 + NY - 1 + 2)
 
-    for s in range(2 * parts):
+    straight = [s for s in range(2 * parts) if s != TURN_G]
+    gq[zx, y] = own[TURN_G]
+
+    def turn_y(d):
+        return pltpu.make_async_remote_copy(
+            src_ref=own.at[TURN_G], dst_ref=gq.at[zx, y],
+            send_sem=q_s.at[0], recv_sem=q_r.at[0],
+            device_id=y_dev(d)[0], device_id_type=MESH,
+        )
+
+    for d in (2, 1, 3):
+        turn_y(d).start()
+
+    for s in straight:
 
         def send(d, _, s=s):
             pltpu.make_async_remote_copy(
@@ -87,6 +110,38 @@
             return 0
 
         lax.fori_loop(1, ROW, send, 0)
+
+    def turn_zx():
+        some = gq.at[0, pl.ds(0, NY - 1)]
+        pltpu.make_async_copy(some, some, q_r.at[0]).wait()
+
+        def send(d, _):
+            pltpu.make_async_remote_copy(
+                src_ref=gq.at[zx], dst_ref=gq.at[zx], send_sem=q_s.at[1], recv_sem=q_r.at[1],
+                device_id=zx_dev(d)[0], device_id_type=MESH,
+            ).start()
+            return 0
+
+        lax.fori_loop(1, ROW, send, 0)
+
+    def turn_sib():
+        rows = pl.ds(pl.multiple_of(c * HALF, HALF), HALF)
+        ref = whole.at[TURN_G // parts, rows, pl.ds((TURN_G % parts) * wide, wide)]
+        return pltpu.make_async_remote_copy(
+            src_ref=ref, dst_ref=ref, send_sem=q_s.at[2], recv_sem=q_r.at[2],
+            device_id=sib, device_id_type=MESH,
+        )
+
+    def turn_in():
+        some = gq.at[pl.ds(0, ROW - 1)]
+        pltpu.make_async_copy(some, some, q_r.at[1]).wait()
+        for yy in range(NY):
+            turned = jnp.swapaxes(gq[:, yy], 0, 1)
+            rows = pl.ds(pl.multiple_of(c * HALF + yy * ROW, ROW), ROW)
+            for k in range(ROW):
+                col = (TURN_G % parts) * wide + k * 128
+                whole[TURN_G // parts, rows, pl.ds(col, 128)] = turned[k]
+        turn_sib().start()
 
     def block(ref, s, yy, cc):
         rows = pl.ds(pl.multiple_of(cc * HALF + yy * ROW, ROW), ROW)
@@ -137,19 +192,18 @@
             device_id=pair, device_id_type=MESH,
         )
 
-    gather_zx(0)
-    gather_zx(1)
+    turn_zx()
+    for s in straight:
+        gather_zx(s)
     gather_y(0)
-    gather_zx(2)
-    gather_y(1)
+    turn_in()
+    gather_y(2)
     gather_sib(0)
     loads[0].wait()
     loads[1].wait()
     gate = nt(piece(wv, 0, 0), piece(whole, 0, 0))
     up = nt(piece(wv, 1, 0), piece(whole, 0, 0))
-    gather_zx(3)
-    gather_y(2)
-    gather_sib(1)
+    turn_sib().wait_recv()
     gate += nt(piece(wv, 0, 1), piece(whole, 0, 1))
     wis[0] = gate.astype(BF)
     to_pair(0).start()
@@ -164,8 +218,6 @@
     dhid += nt(piece(wv, 2, 3), piece(whole, 1, 3))
     wis[2] = dhid.astype(BF)
     to_pair(2).start()
-    saved = [pltpu.make_async_copy(whole, all_out, out_sem.at[0])]
-    saved[0].start()
 
     to_pair(0).wait_recv()
     to_pair(1).wait_recv()
@@ -174,7 +226,6 @@
     sig = jax.nn.sigmoid(gate)
     act = gate * sig
     hidden = (act * up).astype(BF)
-    acts[0] = hidden
     tp[0] = jnp.transpose(hidden.astype(F32)).astype(BF)
 
     rows_own = pl.ds(pl.multiple_of(c * HALF, HALF), HALF)
@@ -186,18 +237,18 @@
             recv_sem=c_r.at[a, h], device_id=sib, device_id_type=MESH,
         )
 
-    def term(a, h):
+    def term(a, h, rows):
         cols = pl.ds(h * wide, wide)
-        for part, rows in ((0, rows_sib), (1, rows_own)):
-            if a == 0:
-                value = nn(tp[0, rows, :], wv[2, :, cols])
-            else:
-                value = nn(tp[1, rows, :], wv[0, :, cols]) + nn(tp[2, rows, :], wv[1, :, cols])
-            if part == 0:
-                cs[a, h] = value.astype(BF)
-                to_core(a, h).start()
-            else:
-                mine[a, h] = value
+        if a == 0:
+            return nn(tp[0, rows, :], wv[2, :, cols])
+        return nn(tp[1, rows, :], wv[0, :, cols]) + nn(tp[2, rows, :], wv[1, :, cols])
+
+    def terms(a):
+        for h in range(parts):
+            cs[a, h] = term(a, h, rows_sib).astype(BF)
+            to_core(a, h).start()
+        for h in range(parts):
+            mine[a, h] = term(a, h, rows_own)
 
     def to_row(a, h, d):
         there = pl.ds(pl.multiple_of(lax.rem(y + d, NY) * ROW, ROW), ROW)
@@ -205,10 +256,46 @@
             src_ref=ys.at[a, h, there], dst_ref=yr.at[a, h, d - 1], send_sem=ry_s.at[a, h, d - 1],
             recv_sem=ry_r.at[a, h, d - 1], device_id=y_dev(d)[0], device_id_type=MESH,
         )
+
+    def split(value):
+        pieces = [value[:, k * 128 : (k + 1) * 128].reshape(1, ROW, 128) for k in range(ROW)]
+        return jnp.swapaxes(jnp.concatenate(pieces, axis=0), 0, 1)
+
+    def turn_out(value):
+        for yy in range(NY):
+            sq[:, yy] = split(value[yy * ROW : (yy + 1) * ROW])
+        rq[0] = sq[zx]
+
+        def send(d, _):
+            there, t = zx_dev(d)
+            pltpu.make_async_remote_copy(
+                src_ref=sq.at[t], dst_ref=rq.at[d], send_sem=qs_s.at[0], recv_sem=qs_r.at[0],
+                device_id=there, device_id_type=MESH,
+            ).start()
+            return 0
+
+        lax.fori_loop(1, ROW, send, 0)
+
+    def turn_back(d):
+        return pltpu.make_async_remote_copy(
+            src_ref=uq.at[lax.rem(y + d, NY)], dst_ref=vq.at[d], send_sem=qy_s.at[d - 1],
+            recv_sem=qy_r.at[d - 1], device_id=y_dev(d)[0], device_id_type=MESH,
+        )
+
+    def turn_sum():
+        some = rq.at[pl.ds(1, ROW - 1)]
+        pltpu.make_async_copy(some, some, qs_r.at[0]).wait()
+        uq[...] = jnp.sum(rq[...].astype(F32), axis=0).astype(BF)
+        for d in (2, 1, 3):
+            turn_back(d).start()
+        vq[0] = uq[y]
 
     def scatter_core(a, h):
         to_core(a, h).wait_recv()
         value = mine[a, h] + cr[a, h].astype(F32)
+        if (a, h) == TURN_S:
+            turn_out(value.astype(BF))
+            return
         mine[a, h] = value
         ys[a, h] = value.astype(BF)
         for d in (2, 1, 3):
@@ -221,10 +308,7 @@
             to_row(a, h, d).wait_recv()
             value = value + yr[a, h, d - 1].astype(F32)
         value = value.astype(BF)
-        split = jnp.concatenate(
-            [value[:, k * 128 : (k + 1) * 128].reshape(1, ROW, 128) for k in range(ROW)], axis=0
-        )
-        zs[a, h] = jnp.swapaxes(split, 0, 1)
+        zs[a, h] = split(value)
         zr[a, h, 0] = zs[a, h, zx]
 
         def send(d, _):
@@ -238,66 +322,83 @@
         lax.fori_loop(1, ROW, send, 0)
 
     def scatter_zx(a, h):
-        some = zr.at[a, h, pl.ds(1, ROW - 1)]
-        pltpu.make_async_copy(some, some, rz_r.at[a, h]).wait()
-        rows_out[a, h * ROW : (h + 1) * ROW, :] = jnp.sum(zr[a, h].astype(F32), axis=0)
-
-    term(0, 0)
-    term(0, 1)
+        if (a, h) == TURN_S:
+            for d in (1, 3, 2):
+                turn_back(d).wait_recv()
+            total = jnp.sum(vq[...].astype(F32), axis=0).astype(BF)
+        else:
+            some = zr.at[a, h, pl.ds(1, ROW - 1)]
+            pltpu.make_async_copy(some, some, rz_r.at[a, h]).wait()
+            total = jnp.sum(zr[a, h].astype(F32), axis=0).astype(BF)
+        for k in range(ROW):
+            col = h * wide + k * 128
+            (out_ref, gin_ref)[a][:, col : col + 128] = total[k : k + 1, :]
+
+    def grad(ref, act_value, a):
+        for j in range(width // 1024):
+            cols = pl.ds(j * 1024, 1024)
+            ref[:, cols] = nn(act_value, whole[a, :, cols]).astype(BF)
+
+    terms(0)
+    scatter_core(0, 0)
+    scatter_core(0, 1)
     to_pair(2).wait_recv()
     dhid = dhid + wir[2].astype(F32)
     dgate = (dhid * up * sig * (1.0 + gate * (1.0 - sig))).astype(BF)
     dup = (dhid * act).astype(BF)
-    acts[1] = dgate
-    acts[2] = dup
-    saved.append(pltpu.make_async_copy(acts, act_out, out_sem.at[1]))
-    saved[1].start()
     tp[1] = jnp.transpose(dgate.astype(F32)).astype(BF)
     tp[2] = jnp.transpose(dup.astype(F32)).astype(BF)
-    scatter_core(0, 0)
-    term(1, 0)
-    scatter_core(0, 1)
-    term(1, 1)
-    scatter_core(1, 0)
-    scatter_core(1, 1)
+    terms(1)
+    for h in range(parts):
+        scatter_core(1, h)
     scatter_y(0, 0)
-    scatter_y(0, 1)
+    turn_sum()
     scatter_y(1, 0)
     scatter_y(1, 1)
+    grad(gd_ref, hidden, 1)
+    grad(gg_ref, dgate, 0)
+    grad(gu_ref, dup, 0)
     for a in range(2):
         for h in range(parts):
             scatter_zx(a, h)
 
-    for s in range(2 * parts):
+    for s in straight:
         some = zxb.at[s, pl.ds(0, ROW - 1)]
         pltpu.make_async_copy(some, some, zx_s.at[s]).wait()
         for d in range(1, NY):
             to_y(s, d).wait_send()
         for d in range(NY):
             to_sib(s, d).wait_send()
+    some = gq.at[0, pl.ds(0, NY - 1)]
+    pltpu.make_async_copy(some, some, q_s.at[0]).wait()
+    some = gq.at[pl.ds(0, ROW - 1)]
+    pltpu.make_async_copy(some, some, q_s.at[1]).wait()
+    turn_sib().wait_send()
     for i in range(3):
         to_pair(i).wait_send()
     for a in range(2):
         for h in range(parts):
             to_core(a, h).wait_send()
+            if (a, h) == TURN_S:
+                some = sq.at[pl.ds(0, ROW - 1)]
+                pltpu.make_async_copy(some, some, qs_s.at[0]).wait()
+                for d in range(1, NY):
+                    turn_back(d).wait_send()
+                continue
             for d in range(1, NY):
                 to_row(a, h, d).wait_send()
             some = zs.at[a, h, pl.ds(0, ROW - 1)]
             pltpu.make_async_copy(some, some, rz_s.at[a, h]).wait()
-    for copy in saved:
+
+
+def store_kernel(*refs):
+    sems = refs[-1]
+    n = (len(refs) - 1) // 2
+    copies = [pltpu.make_async_copy(refs[i], refs[n + i], sems.at[i]) for i in range(n)]
+    for copy in copies:
+        copy.start()
+    for copy in copies:
         copy.wait()
-
-
-def grads_kernel(all_ref, act_ref, rows_ref, out_ref, gin_ref, gg_ref, gu_ref, gd_ref):
-    gd_ref[...] = nn(act_ref[0], all_ref[1]).astype(BF)
-    gg_ref[...] = nn(act_ref[1], all_ref[0]).astype(BF)
-    gu_ref[...] = nn(act_ref[2], all_ref[0]).astype(BF)
-
-    @pl.when(pl.program_id(0) == 0)
-    def _():
-        for a, ref in enumerate((out_ref, gin_ref)):
-            for k in range(rows_ref.shape[1]):
-                ref[:, k * 128 : (k + 1) * 128] = rows_ref[a, k : k + 1, :].astype(BF)
 
 
 def per_device(tokens, gate_weight, up_weight, down_weight, cotangent):
@@ -307,18 +408,17 @@
     parts = width // wide
     st = 2 * parts
     vm = pl.BlockSpec(memory_space=pltpu.VMEM)
-    hbm = pl.BlockSpec(memory_space=pl.ANY)
+    hbm = pl.BlockSpec(memory_space=pltpu.HBM)
     sem = pltpu.SemaphoreType.DMA
-    whole, acts, rows = pl.pallas_call(
+    shapes = [jax.ShapeDtypeStruct((1, width), BF)] * 2
+    shapes += [jax.ShapeDtypeStruct((units, width), BF)] * 3
+    results = pl.pallas_call(
         exchange_kernel,
-        out_shape=[
-            jax.ShapeDtypeStruct((2, tokens_all, width), BF),
-            jax.ShapeDtypeStruct((3, units, tokens_all), BF),
-            jax.ShapeDtypeStruct((2, width // 128, 128), F32),
-        ],
-        in_specs=[vm, vm, hbm, hbm, hbm],
-        out_specs=[hbm, hbm, vm],
+        out_shape=shapes,
+        in_specs=[hbm] * 5,
+        out_specs=[vm] * 5,
         scratch_shapes=[
+            pltpu.VMEM((2, 1, width), BF),
             pltpu.VMEM((3, units, width), BF),
             pltpu.VMEM((2 * width // 128, 128), F32),
             pltpu.VMEM((st, ROW, 128), BF),
@@ -334,35 +434,33 @@
             pltpu.VMEM((2, parts, NY - 1, ROW, wide), BF),
             pltpu.VMEM((2, parts, ROW, ROW, 128), BF),
             pltpu.VMEM((2, parts, ROW, ROW, 128), BF),
-            pltpu.VMEM((3, units, tokens_all), BF),
-            sem((3,)), sem((st,)), sem((st,)), sem((st, NY - 1)), sem((st, NY - 1)),
+            sem((5,)), sem((st,)), sem((st,)), sem((st, NY - 1)), sem((st, NY - 1)),
             sem((st, NY)), sem((st, NY)), sem((3,)), sem((3,)),
             sem((2, parts)), sem((2, parts)), sem((2, parts, NY - 1)), sem((2, parts, NY - 1)),
-            sem((2, parts)), sem((2, parts)), sem((2,)),
+            sem((2, parts)), sem((2, parts)),
+            pltpu.VMEM((ROW, NY, ROW, 128), BF),
+            pltpu.VMEM((ROW, NY, ROW, 128), BF),
+            pltpu.VMEM((ROW, NY, ROW, 128), BF),
+            pltpu.VMEM((NY, ROW, 128), BF),
+            pltpu.VMEM((NY, ROW, 128), BF),
+            sem((3,)), sem((3,)), sem((1,)), sem((1,)), sem((NY - 1,)), sem((NY - 1,)),
         ],
         compiler_params=pltpu.CompilerParams(
             collective_id=0, has_side_effects=True, vmem_limit_bytes=48 << 20
         ),
         name="exchange",
     )(tokens, cotangent, gate_weight, up_weight, down_weight)
-    step = 512
-    big = pl.BlockSpec((units, step), lambda j: (0, j))
-    small = pl.BlockSpec((1, width), lambda j: (0, 0))
-    output, grad_input, grad_gate, grad_up, grad_down = pl.pallas_call(
-        grads_kernel,
-        grid=(width // step,),
-        out_shape=[jax.ShapeDtypeStruct((1, width), BF)] * 2
-        + [jax.ShapeDtypeStruct((units, width), BF)] * 3,
-        in_specs=[
-            pl.BlockSpec((2, tokens_all, step), lambda j: (0, 0, j)),
-            pl.BlockSpec((3, units, tokens_all), lambda j: (0, 0, 0)),
-            pl.BlockSpec((2, width // 128, 128), lambda j: (0, 0, 0)),
-        ],
-        out_specs=[small, small, big, big, big],
-        compiler_params=pltpu.CompilerParams(vmem_limit_bytes=48 << 20),
-        name="grads",
-    )(whole, acts, rows)
-    return output, grad_input, grad_gate, grad_up, grad_down
+    return tuple(
+        pl.pallas_call(
+            store_kernel,
+            out_shape=shapes,
+            in_specs=[vm] * 5,
+            out_specs=[hbm] * 5,
+            scratch_shapes=[sem((5,))],
+            compiler_params=pltpu.CompilerParams(vmem_limit_bytes=1 << 20),
+            name="store",
+        )(*results)
+    )
 
 
 def solution(mesh):

time: 71.9 us -> 57.7 us (0.80)
  Pallas kernels: 63.4 us -> 55.3 us
  local copies, waits for them, and re-layouts: 7.51 us -> 1.43 us
    pallas_call x2, Pallas kernels: 63.4 us -> 55.3 us  [the longest x1 52.9 us: per_device(): pl.pallas_call(exchange_kernel, out_shape=shapes, in_specs=[hbm] * 5, out...]
    unnamed x12 -> x4, local copies, waits for them, and re-layouts: 7.51 us -> 1.43 us
where the time goes in v2:
time: 57.7 us; the launch traced here: 57.4 us
  Pallas kernels  55.3 us (96%)
  local copies, waits for them, and re-layouts  1.43 us (2%)
  between operations  0.65 us (1%)
    pallas_call x1, Pallas kernels, per_device(): pl.pallas_call(exchange_kernel, out_shape=shapes, in_specs=[hbm] * 5, out...  52.9 us
    pallas_call x1, Pallas kernels, per_device(): pl.pallas_call(store_kernel, out_shape=shapes, in_specs=[vm] * 5, out_spe...  2.49 us
    unnamed x4, local copies, waits for them, and re-layouts  1.43 us

profile of v2, /device:TPU:1, one launch (start us, length us, event | category | flops | bytes accessed | tf_op | source)
XLA Modules:
  0.0 57.4 jit_solution(4419273187609902157)
XLA Ops:
  0.6 0.0 copy-start
  0.6 0.7 %copy-done = bf16[1,4096]{1,0:T(2,128)(2,1)S(1)} copy-done((bf16[1,4096]{1,0:T(2,128)(2,1)S(1)}, bf16[1,4096]{1,0:T(2,128)(2,1)}, u32[]{:S(2)}) %copy-start) | copy-done | bytes 8216
  1.4 0.0 copy-start.1
  1.4 0.7 %copy-done.1 = bf16[1,4096]{1,0:T(2,128)(2,1)S(1)} copy-done((bf16[1,4096]{1,0:T(2,128)(2,1)S(1)}, bf16[1,4096]{1,0:T(2,128)(2,1)}, u32[]{:S(2)}) %copy-start.1) | copy-done | bytes 8216
  2.1 52.9 %exchange.1 = (bf16[1,4096]{1,0:T(2,128)(2,1)S(1)}, bf16[1,4096]{1,0:T(2,128)(2,1)S(1)}, bf16[224,4096]{1,0:T(8,128)(2,1)S(1)}, bf16[224,4096]{1,0:T(8,128)(2,1)S(1)}, bf16[224,4096]{1,0:T(8,128)(2,1)S(1)}) custom-call(bf16[1,4096]{1,0:T(2,128)(2,1)S(1)} %copy-done, bf16[1,4096]{1,0:T(2,128)(2,1)S(1)} %copy-done.1, bf16[224,4096]{1,0:T(8,128)(2,1)} %gw_hbm.1, ...), custom_call_target="tpu_custom_call" | custom-call | tf_op jit(solution)/shard_map/exchange/pallas_call | solution.py:415
  54.9 2.5 %store.1 = (bf16[1,4096]{1,0:T(2,128)(2,1)}, bf16[1,4096]{1,0:T(2,128)(2,1)}, bf16[224,4096]{1,0:T(8,128)(2,1)}, bf16[224,4096]{1,0:T(8,128)(2,1)}, bf16[224,4096]{1,0:T(8,128)(2,1)}) custom-call(bf16[1,4096]{1,0:T(2,128)(2,1)S(1)} %get-tuple-element.10.refs_0_, bf16[1,4096]{1,0:T(2,128)(2,1)S(1)} %get-tuple-element.11.refs_1_, ...), custom_call_target="tpu_custom_call" | custom-call | tf_op jit(solution)/shard_map/store/pallas_call | solution.py:454
Async XLA Ops:
  0.6 0.7 %copy-start = (bf16[1,4096]{1,0:T(2,128)(2,1)S(1)}, bf16[1,4096]{1,0:T(2,128)(2,1)}, u32[]{:S(2)}) copy-start(bf16[1,4096]{1,0:T(2,128)(2,1)} %tok_hbm.1) | copy-start | bytes 24580
  1.4 0.7 %copy-start.1 = (bf16[1,4096]{1,0:T(2,128)(2,1)S(1)}, bf16[1,4096]{1,0:T(2,128)(2,1)}, u32[]{:S(2)}) copy-start(bf16[1,4096]{1,0:T(2,128)(2,1)} %cot_hbm.1) | copy-start | bytes 24580

commit v3 on v2

--- a/solution.py
+++ b/solution.py
@@ -28,12 +28,12 @@
 def exchange_kernel(
     tok_hbm, cot_hbm, gw_hbm, uw_hbm, dw_hbm,
     out_ref, gin_ref, gg_ref, gu_ref, gd_ref,
-    raw, wv, own32, own, zxb, whole, wis, wir, tp, cs, cr, mine, ys, yr, zs, zr,
-    w_sem, zx_s, zx_r, y_s, y_r, sib_s, sib_r, wi_s, wi_r,
-    c_s, c_r, ry_s, ry_r, rz_s, rz_r,
+    raw, wv, own32, own, zxb, whole, wis, wir, acts, gact, mine, ys, yr, zs, zr,
+    w_sem, zx_s, zx_r, y_s, y_r, sw_s, sw_r, st_s, st_r, sa_s, sa_r, wi_s, wi_r,
+    ry_s, ry_r, rz_s, rz_r,
     gq, sq, rq, uq, vq, q_s, q_r, qs_s, qs_r, qy_s, qy_r,
 ):
-    width = wv.shape[2]
+    width = wv.shape[3]
     parts = width // (ROW * 128)
     wide = ROW * 128
     tok_i, wi_i, wo_i = lax.axis_index("tok"), lax.axis_index("wi"), lax.axis_index("wo")
@@ -56,7 +56,7 @@
         pltpu.make_async_copy(w, there, w_sem.at[i])
         for i, (w, there) in enumerate(
             (
-                (gw_hbm, wv.at[0]), (uw_hbm, wv.at[1]), (dw_hbm, wv.at[2]),
+                (gw_hbm, wv.at[0, c]), (uw_hbm, wv.at[1, c]), (dw_hbm, wv.at[2, c]),
                 (tok_hbm, raw.at[0]), (cot_hbm, raw.at[1]),
             )
         )
@@ -124,14 +124,6 @@
 
         lax.fori_loop(1, ROW, send, 0)
 
-    def turn_sib():
-        rows = pl.ds(pl.multiple_of(c * HALF, HALF), HALF)
-        ref = whole.at[TURN_G // parts, rows, pl.ds((TURN_G % parts) * wide, wide)]
-        return pltpu.make_async_remote_copy(
-            src_ref=ref, dst_ref=ref, send_sem=q_s.at[2], recv_sem=q_r.at[2],
-            device_id=sib, device_id_type=MESH,
-        )
-
     def turn_in():
         some = gq.at[pl.ds(0, ROW - 1)]
         pltpu.make_async_copy(some, some, q_r.at[1]).wait()
@@ -141,7 +133,6 @@
             for k in range(ROW):
                 col = (TURN_G % parts) * wide + k * 128
                 whole[TURN_G // parts, rows, pl.ds(col, 128)] = turned[k]
-        turn_sib().start()
 
     def block(ref, s, yy, cc):
         rows = pl.ds(pl.multiple_of(cc * HALF + yy * ROW, ROW), ROW)
@@ -154,13 +145,22 @@
             device_id=y_dev(d)[0], device_id_type=MESH,
         )
 
-    def to_sib(s, d):
-        yy = lax.rem(y + NY - d, NY)
-        return pltpu.make_async_remote_copy(
-            src_ref=block(whole, s, yy, c), dst_ref=block(whole, s, yy, c),
-            send_sem=sib_s.at[s, d], recv_sem=sib_r.at[s, d],
-            device_id=sib, device_id_type=MESH,
-        )
+    rows_own = pl.ds(pl.multiple_of(c * HALF, HALF), HALF)
+
+    def to_sib(ref, send_sem, recv_sem, there=None):
+        return pltpu.make_async_remote_copy(
+            src_ref=ref, dst_ref=ref if there is None else there, send_sem=send_sem,
+            recv_sem=recv_sem, device_id=sib, device_id_type=MESH,
+        )
+
+    def weights(i):
+        return to_sib(wv.at[i, c], sw_s.at[i], sw_r.at[i])
+
+    def share(a):
+        return to_sib(whole.at[a, rows_own], st_s.at[a], st_r.at[a])
+
+    def share_act(i):
+        return to_sib(acts.at[i, 1 - c], sa_s.at[i], sa_r.at[i], gact.at[i, c])
 
     def gather_zx(s):
         some = zxb.at[s, pl.ds(0, ROW - 1)]
@@ -172,19 +172,30 @@
             whole[s // parts, rows, pl.ds(col, 128)] = turned[k]
         for d in (2, 1, 3):
             to_y(s, d).start()
-        to_sib(s, 0).start()
 
     def gather_y(s):
         for d in (1, 3, 2):
             to_y(s, d).wait_recv()
-            to_sib(s, d).start()
-
-    def gather_sib(s):
-        for d in (0, 1, 3, 2):
-            to_sib(s, d).wait_recv()
-
-    def piece(ref, i, s):
-        return ref[i, :, pl.ds((s % parts) * wide, wide)]
+
+    def dots(i, s):
+        cols = pl.ds((s % parts) * wide, wide)
+        value = whole[s // parts, rows_own, cols]
+        return [nt(value, wv[i, b, :, cols]) for b in range(NC)]
+
+    def add(left, right):
+        return [x + y for x, y in zip(left, right)]
+
+    def give_pair(i, values):
+        for b in range(NC):
+            wis[i, b] = values[b].astype(BF)
+        to_pair(i).start()
+
+    def take_pair(i, values):
+        to_pair(i).wait_recv()
+        return [values[b] + wir[i, b].astype(F32) for b in range(NC)]
+
+    def keep(i, b, value):
+        acts[i, b] = value.astype(BF)
 
     def to_pair(i):
         return pltpu.make_async_remote_copy(
@@ -193,62 +204,45 @@
         )
 
     turn_zx()
+    for i in range(3):
+        loads[i].wait()
+        weights(i).start()
     for s in straight:
         gather_zx(s)
     gather_y(0)
+    weights(0).wait_recv()
+    gate = dots(0, 0)
+    weights(1).wait_recv()
+    up = dots(1, 0)
     turn_in()
+    gate = add(gate, dots(0, 1))
+    give_pair(0, gate)
+    up = add(up, dots(1, 1))
+    give_pair(1, up)
+    share(0).start()
     gather_y(2)
-    gather_sib(0)
-    loads[0].wait()
-    loads[1].wait()
-    gate = nt(piece(wv, 0, 0), piece(whole, 0, 0))
-    up = nt(piece(wv, 1, 0), piece(whole, 0, 0))
-    turn_sib().wait_recv()
-    gate += nt(piece(wv, 0, 1), piece(whole, 0, 1))
-    wis[0] = gate.astype(BF)
-    to_pair(0).start()
-    up += nt(piece(wv, 1, 1), piece(whole, 0, 1))
-    wis[1] = up.astype(BF)
-    to_pair(1).start()
+    weights(2).wait_recv()
+    dhid = dots(2, 2)
     gather_y(3)
-    gather_sib(2)
-    loads[2].wait()
-    dhid = nt(piece(wv, 2, 2), piece(whole, 1, 2))
-    gather_sib(3)
-    dhid += nt(piece(wv, 2, 3), piece(whole, 1, 3))
-    wis[2] = dhid.astype(BF)
-    to_pair(2).start()
-
-    to_pair(0).wait_recv()
-    to_pair(1).wait_recv()
-    gate = gate + wir[0].astype(F32)
-    up = up + wir[1].astype(F32)
-    sig = jax.nn.sigmoid(gate)
-    act = gate * sig
-    hidden = (act * up).astype(BF)
-    tp[0] = jnp.transpose(hidden.astype(F32)).astype(BF)
-
-    rows_own = pl.ds(pl.multiple_of(c * HALF, HALF), HALF)
-    rows_sib = pl.ds(pl.multiple_of((1 - c) * HALF, HALF), HALF)
-
-    def to_core(a, h):
-        return pltpu.make_async_remote_copy(
-            src_ref=cs.at[a, h], dst_ref=cr.at[a, h], send_sem=c_s.at[a, h],
-            recv_sem=c_r.at[a, h], device_id=sib, device_id_type=MESH,
-        )
-
-    def term(a, h, rows):
+    dhid = add(dhid, dots(2, 3))
+    give_pair(2, dhid)
+    share(1).start()
+
+    gate = take_pair(0, gate)
+    up = take_pair(1, up)
+    sig = [jax.nn.sigmoid(v) for v in gate]
+    act = [gate[b] * sig[b] for b in range(NC)]
+    for b in range(NC):
+        keep(0, b, act[b] * up[b])
+
+    def term(a, h):
         cols = pl.ds(h * wide, wide)
-        if a == 0:
-            return nn(tp[0, rows, :], wv[2, :, cols])
-        return nn(tp[1, rows, :], wv[0, :, cols]) + nn(tp[2, rows, :], wv[1, :, cols])
-
-    def terms(a):
-        for h in range(parts):
-            cs[a, h] = term(a, h, rows_sib).astype(BF)
-            to_core(a, h).start()
-        for h in range(parts):
-            mine[a, h] = term(a, h, rows_own)
+        total = None
+        for i, w in ((0, 2),) if a == 0 else ((1, 0), (2, 1)):
+            for b in range(NC):
+                value = nn(acts[i, b], wv[w, b, :, cols])
+                total = value if total is None else total + value
+        return total
 
     def to_row(a, h, d):
         there = pl.ds(pl.multiple_of(lax.rem(y + d, NY) * ROW, ROW), ROW)
@@ -290,9 +284,8 @@
             turn_back(d).start()
         vq[0] = uq[y]
 
-    def scatter_core(a, h):
-        to_core(a, h).wait_recv()
-        value = mine[a, h] + cr[a, h].astype(F32)
+    def scatter_first(a, h):
+        value = term(a, h)
         if (a, h) == TURN_S:
             turn_out(value.astype(BF))
             return
@@ -334,30 +327,35 @@
             col = h * wide + k * 128
             (out_ref, gin_ref)[a][:, col : col + 128] = total[k : k + 1, :]
 
-    def grad(ref, act_value, a):
+    def grad(ref, i, a):
+        share_act(i).wait_recv()
+        gact[i, c] = acts[i, c]
+        both = jnp.concatenate([gact[i, b] for b in range(NC)], axis=0)
+        act_value = jnp.transpose(both.astype(F32)).astype(BF)
         for j in range(width // 1024):
             cols = pl.ds(j * 1024, 1024)
             ref[:, cols] = nn(act_value, whole[a, :, cols]).astype(BF)
 
-    terms(0)
-    scatter_core(0, 0)
-    scatter_core(0, 1)
-    to_pair(2).wait_recv()
-    dhid = dhid + wir[2].astype(F32)
-    dgate = (dhid * up * sig * (1.0 + gate * (1.0 - sig))).astype(BF)
-    dup = (dhid * act).astype(BF)
-    tp[1] = jnp.transpose(dgate.astype(F32)).astype(BF)
-    tp[2] = jnp.transpose(dup.astype(F32)).astype(BF)
-    terms(1)
-    for h in range(parts):
-        scatter_core(1, h)
+    scatter_first(0, 0)
+    scatter_first(0, 1)
+    share_act(0).start()
+    dhid = take_pair(2, dhid)
+    for b in range(NC):
+        keep(1, b, dhid[b] * up[b] * sig[b] * (1.0 + gate[b] * (1.0 - sig[b])))
+        keep(2, b, dhid[b] * act[b])
+    scatter_first(1, 0)
+    scatter_first(1, 1)
+    share_act(1).start()
+    share_act(2).start()
     scatter_y(0, 0)
     turn_sum()
     scatter_y(1, 0)
     scatter_y(1, 1)
-    grad(gd_ref, hidden, 1)
-    grad(gg_ref, dgate, 0)
-    grad(gu_ref, dup, 0)
+    for a in range(2):
+        share(a).wait_recv()
+    grad(gd_ref, 0, 1)
+    grad(gg_ref, 1, 0)
+    grad(gu_ref, 2, 0)
     for a in range(2):
         for h in range(parts):
             scatter_zx(a, h)
@@ -367,18 +365,18 @@
         pltpu.make_async_copy(some, some, zx_s.at[s]).wait()
         for d in range(1, NY):
             to_y(s, d).wait_send()
-        for d in range(NY):
-            to_sib(s, d).wait_send()
     some = gq.at[0, pl.ds(0, NY - 1)]
     pltpu.make_async_copy(some, some, q_s.at[0]).wait()
     some = gq.at[pl.ds(0, ROW - 1)]
     pltpu.make_async_copy(some, some, q_s.at[1]).wait()
-    turn_sib().wait_send()
     for i in range(3):
         to_pair(i).wait_send()
+        weights(i).wait_send()
+        share_act(i).wait_send()
+    for a in range(2):
+        share(a).wait_send()
     for a in range(2):
         for h in range(parts):
-            to_core(a, h).wait_send()
             if (a, h) == TURN_S:
                 some = sq.at[pl.ds(0, ROW - 1)]
                 pltpu.make_async_copy(some, some, qs_s.at[0]).wait()
@@ -412,6 +410,7 @@
     sem = pltpu.SemaphoreType.DMA
     shapes = [jax.ShapeDtypeStruct((1, width), BF)] * 2
     shapes += [jax.ShapeDtypeStruct((units, width), BF)] * 3
+    inputs = (tokens, cotangent, gate_weight, up_weight, down_weight)
     results = pl.pallas_call(
         exchange_kernel,
         out_shape=shapes,
@@ -419,37 +418,36 @@
         out_specs=[vm] * 5,
         scratch_shapes=[
             pltpu.VMEM((2, 1, width), BF),
-            pltpu.VMEM((3, units, width), BF),
+            pltpu.VMEM((3, NC, units, width), BF),
             pltpu.VMEM((2 * width // 128, 128), F32),
             pltpu.VMEM((st, ROW, 128), BF),
             pltpu.VMEM((st, ROW, ROW, 128), BF),
             pltpu.VMEM((2, tokens_all, width), BF),
-            pltpu.VMEM((3, units, tokens_all), BF),
-            pltpu.VMEM((3, units, tokens_all), BF),
-            pltpu.VMEM((3, tokens_all, units), BF),
-            pltpu.VMEM((2, parts, HALF, wide), BF),
-            pltpu.VMEM((2, parts, HALF, wide), BF),
+            pltpu.VMEM((3, NC, HALF, units), BF),
+            pltpu.VMEM((3, NC, HALF, units), BF),
+            pltpu.VMEM((3, NC, HALF, units), BF),
+            pltpu.VMEM((3, NC, HALF, units), BF),
             pltpu.VMEM((2, parts, HALF, wide), F32),
             pltpu.VMEM((2, parts, HALF, wide), BF),
             pltpu.VMEM((2, parts, NY - 1, ROW, wide), BF),
             pltpu.VMEM((2, parts, ROW, ROW, 128), BF),
             pltpu.VMEM((2, parts, ROW, ROW, 128), BF),
             sem((5,)), sem((st,)), sem((st,)), sem((st, NY - 1)), sem((st, NY - 1)),
-            sem((st, NY)), sem((st, NY)), sem((3,)), sem((3,)),
-            sem((2, parts)), sem((2, parts)), sem((2, parts, NY - 1)), sem((2, parts, NY - 1)),
+            sem((3,)), sem((3,)), sem((2,)), sem((2,)), sem((3,)), sem((3,)), sem((3,)), sem((3,)),
+            sem((2, parts, NY - 1)), sem((2, parts, NY - 1)),
             sem((2, parts)), sem((2, parts)),
             pltpu.VMEM((ROW, NY, ROW, 128), BF),
             pltpu.VMEM((ROW, NY, ROW, 128), BF),
             pltpu.VMEM((ROW, NY, ROW, 128), BF),
             pltpu.VMEM((NY, ROW, 128), BF),
             pltpu.VMEM((NY, ROW, 128), BF),
-            sem((3,)), sem((3,)), sem((1,)), sem((1,)), sem((NY - 1,)), sem((NY - 1,)),
+            sem((2,)), sem((2,)), sem((1,)), sem((1,)), sem((NY - 1,)), sem((NY - 1,)),
         ],
         compiler_params=pltpu.CompilerParams(
             collective_id=0, has_side_effects=True, vmem_limit_bytes=48 << 20
         ),
         name="exchange",
-    )(tokens, cotangent, gate_weight, up_weight, down_weight)
+    )(*[pltpu.with_memory_space_constraint(x, pltpu.HBM) for x in inputs])
     return tuple(
         pl.pallas_call(
             store_kernel,

time: 57.7 us -> 51.2 us (0.89)
  Pallas kernels: 55.3 us -> 50.4 us
  local copies, waits for them, and re-layouts: 1.43 us -> 0 us
    pallas_call x1, Pallas kernels: 52.9 us -> 47.9 us  [per_device(): pl.pallas_call(exchange_kernel, out_shape=shapes, in_specs=[hbm] * 5, out...]
    unnamed x4 -> x0, local copies, waits for them, and re-layouts: 1.43 us -> none
where the time goes in v3:
time: 51.2 us; the launch traced here: 51 us
  Pallas kernels  50.4 us (98%)
  between operations  0.64 us (1%)
    pallas_call x1, Pallas kernels, per_device(): pl.pallas_call(exchange_kernel, out_shape=shapes, in_specs=[hbm] * 5, out...  47.9 us
    pallas_call x1, Pallas kernels, per_device(): pl.pallas_call(store_kernel, out_shape=shapes, in_specs=[vm] * 5, out_spe...  2.49 us

profile of v3, /device:TPU:1, one launch (start us, length us, event | category | flops | bytes accessed | tf_op | source)
XLA Modules:
  0.0 51.0 jit_solution(1961616042325428616)
XLA Ops:
  0.6 47.9 %exchange.1 = (bf16[1,4096]{1,0:T(2,128)(2,1)S(1)}, bf16[1,4096]{1,0:T(2,128)(2,1)S(1)}, bf16[224,4096]{1,0:T(8,128)(2,1)S(1)}, bf16[224,4096]{1,0:T(8,128)(2,1)S(1)}, bf16[224,4096]{1,0:T(8,128)(2,1)S(1)}) custom-call(bf16[1,4096]{1,0:T(2,128)(2,1)} %tok_hbm.1, bf16[1,4096]{1,0:T(2,128)(2,1)} %cot_hbm.1, bf16[224,4096]{1,0:T(8,128)(2,1)} %gw_hbm.1, ...), custom_call_target="tpu_custom_call" | custom-call | tf_op jit(solution)/shard_map/exchange/pallas_call | solution.py:414
  48.5 2.5 %store.1 = (bf16[1,4096]{1,0:T(2,128)(2,1)}, bf16[1,4096]{1,0:T(2,128)(2,1)}, bf16[224,4096]{1,0:T(8,128)(2,1)}, bf16[224,4096]{1,0:T(8,128)(2,1)}, bf16[224,4096]{1,0:T(8,128)(2,1)}) custom-call(bf16[1,4096]{1,0:T(2,128)(2,1)S(1)} %get-tuple-element.10.refs_0_, bf16[1,4096]{1,0:T(2,128)(2,1)S(1)} %get-tuple-element.11.refs_1_, ...), custom_call_target="tpu_custom_call" | custom-call | tf_op jit(solution)/shard_map/store/pallas_call | solution.py:452

commit v4 on v3

--- a/solution.py
+++ b/solution.py
@@ -14,7 +14,7 @@
 ROW = NZ * NX
 HALF = NY * ROW
 TURN_G = 1
-TURN_S = (0, 1)
+TURN_S = (1, 0)
 
 
 def nt(left, right):
@@ -348,9 +348,9 @@
     share_act(1).start()
     share_act(2).start()
     scatter_y(0, 0)
+    scatter_y(0, 1)
+    scatter_y(1, 1)
     turn_sum()
-    scatter_y(1, 0)
-    scatter_y(1, 1)
     for a in range(2):
         share(a).wait_recv()
     grad(gd_ref, 0, 1)

time: 51.2 us -> 50.6 us (0.988); the launches traced: 51 us -> 49.8 us
  Pallas kernels: 50.4 us -> 49.1 us
    pallas_call x1, Pallas kernels: 47.9 us -> 46.6 us  [per_device(): pl.pallas_call(exchange_kernel, out_shape=shapes, in_specs=[hbm] * 5, out...]
where the time goes in v4:
time: 50.6 us; the launch traced here: 49.8 us
  Pallas kernels  49.1 us (97%)
  between operations  0.64 us (1%)
    pallas_call x1, Pallas kernels, per_device(): pl.pallas_call(exchange_kernel, out_shape=shapes, in_specs=[hbm] * 5, out...  46.6 us
    pallas_call x1, Pallas kernels, per_device(): pl.pallas_call(store_kernel, out_shape=shapes, in_specs=[vm] * 5, out_spe...  2.49 us

profile of v4, /device:TPU:1, one launch (start us, length us, event | category | flops | bytes accessed | tf_op | source)
XLA Modules:
  0.0 49.8 jit_solution(5345913342991926405)
XLA Ops:
  0.6 46.6 %exchange.1 = (bf16[1,4096]{1,0:T(2,128)(2,1)S(1)}, bf16[1,4096]{1,0:T(2,128)(2,1)S(1)}, bf16[224,4096]{1,0:T(8,128)(2,1)S(1)}, bf16[224,4096]{1,0:T(8,128)(2,1)S(1)}, bf16[224,4096]{1,0:T(8,128)(2,1)S(1)}) custom-call(bf16[1,4096]{1,0:T(2,128)(2,1)} %tok_hbm.1, bf16[1,4096]{1,0:T(2,128)(2,1)} %cot_hbm.1, bf16[224,4096]{1,0:T(8,128)(2,1)} %gw_hbm.1, ...), custom_call_target="tpu_custom_call" | custom-call | tf_op jit(solution)/shard_map/exchange/pallas_call | solution.py:414
  47.3 2.5 %store.1 = (bf16[1,4096]{1,0:T(2,128)(2,1)}, bf16[1,4096]{1,0:T(2,128)(2,1)}, bf16[224,4096]{1,0:T(8,128)(2,1)}, bf16[224,4096]{1,0:T(8,128)(2,1)}, bf16[224,4096]{1,0:T(8,128)(2,1)}) custom-call(bf16[1,4096]{1,0:T(2,128)(2,1)S(1)} %get-tuple-element.10.refs_0_, bf16[1,4096]{1,0:T(2,128)(2,1)S(1)} %get-tuple-element.11.refs_1_, ...), custom_call_target="tpu_custom_call" | custom-call | tf_op jit(solution)/shard_map/store/pallas_call | solution.py:452
